TPU v7x, 32 devices: a whole 2x2x4 slice. The times are simulated.
32 devices in a mesh: patch: 2 (over y), visit: 4 (over z), tile: 4 (over x, core).
Axes of the slice: x: 2, y: 2, z: 4, core: 2. Of those that a mesh axis runs over, the one named last changes fastest.
Arguments:
- exposure: float32 [16, 256, 4096], P('visit', ('patch', 'tile')), parts along dimension 1, may hold values from -12 to 12
- variance: float32 [16, 256, 4096], P('visit', ('patch', 'tile')), parts along dimension 1, may hold values from 0.25 to 4
- usable: int32 [16, 256, 4096], P('visit', ('patch', 'tile')), parts along dimension 1, may hold values from 0 to 1, as said below
- basis_width: float32 [32, 3], P(('patch', 'visit')), parts along dimension 0, may hold values from 0.8 to 3.5
- spatial_coef: float32 [32, 3, 6], P(('patch', 'visit')), parts along dimension 0, may hold values from -0.6 to 1.4
Outputs:
- coadd: float32 [256, 4096], P(('patch', 'tile')), parts along dimension 0
There are 2 independent parts, one for each index of `patch`. A program takes and returns all parts, laid end to end along the dimension named above; each array names one. Nothing has to cross between parts.
Inputs may be any that keep to these rules, and one draw needn't show every extreme that they name: 1 marks a usable sample; at every pixel at least 5 of the 16 visits are usable.
All inputs are finite; a program needn't handle non-finite values.
Results may differ from a plain program's by a relative error of at most 0.0003.
Values sent between devices are 32-bit elements; how exact they have to be, the bound alone decides.
A program may use at most 128 MiB of HBM per device.

v0:
```python
import jax
import jax.numpy as jnp
from jax import lax
from jax.sharding import PartitionSpec as P

KHALF = 15
BASES = 3


big_value = 1e30


def with_halo(cells, sides, width):
    for axis, dim in sides:
        count = lax.axis_size(axis)
        ends = count - 1
        head = lax.slice_in_dim(cells, 0, width, axis=dim)
        tail = lax.slice_in_dim(cells, cells.shape[dim] - width, cells.shape[dim], axis=dim)
        cells = jnp.concatenate(
            [
                lax.ppermute(tail, axis, [(i, (i + 1) % count) for i in range(ends)]),
                cells,
                lax.ppermute(head, axis, [((i + 1) % count, i) for i in range(ends)]),
            ],
            axis=dim,
        )
    return cells


def combined_all(array, axis, combine):
    everything = jax.tree.map(lambda part: lax.all_gather(part, axis), array)
    initial = jax.tree.map(lambda part: part[0], everything)

    def step(k, so_far):
        return combine(so_far, jax.tree.map(lambda part: part[k], everything))

    return lax.fori_loop(1, lax.axis_size(axis), step, initial)


def basis_profile(offsets, width, basis_id):
    profile = jnp.exp(-offsets * offsets / (2.0 * width * width))
    if basis_id > 0:
        profile = profile * (offsets / width) ** (2 * basis_id)
    return profile


def merge_records(first, second):
    smallest = jnp.minimum(first[0], second[0])
    second_low = jnp.minimum(jnp.minimum(first[1], second[1]), jnp.maximum(first[0], second[0]))
    third_low = jnp.minimum(
        jnp.minimum(first[2], second[2]),
        jnp.minimum(jnp.maximum(first[0], second[1]), jnp.maximum(first[1], second[0])),
    )
    largest = jnp.maximum(first[3], second[3])
    second_high = jnp.maximum(jnp.maximum(first[4], second[4]), jnp.minimum(first[3], second[3]))
    third_high = jnp.maximum(
        jnp.maximum(first[5], second[5]),
        jnp.maximum(jnp.minimum(first[3], second[4]), jnp.minimum(first[4], second[3])),
    )
    return (smallest, second_low, third_low, largest, second_high, third_high)


def band_matrices(offsets_grid, basis_width, totals):
    inside = (jnp.abs(offsets_grid) <= KHALF).astype(jnp.float32)
    matrices = []
    for basis_id in range(BASES):
        widths = basis_width[:, basis_id][:, None, None]
        profile = basis_profile(offsets_grid[None], widths, basis_id)
        matrices.append(profile * inside[None] / totals[:, basis_id][:, None, None])
    return jnp.stack(matrices, axis=1)


def per_device(exposure, variance, usable, basis_width, spatial_coef):
    visits_here, row_count, col_count = exposure.shape
    offsets = jnp.arange(-KHALF, KHALF + 1).astype(jnp.float32)
    totals = jnp.stack(
        [
            jnp.sum(
                basis_profile(offsets[None, :], basis_width[:, basis_id : basis_id + 1], basis_id),
                axis=1,
            )
            for basis_id in range(BASES)
        ],
        axis=1,
    )
    extended = with_halo(exposure, (("tile", 1),), KHALF)
    out_rows = jnp.arange(row_count)[:, None]
    in_rows = jnp.arange(row_count + 2 * KHALF)[None, :]
    vertical_offsets = (in_rows - out_rows - KHALF).astype(jnp.float32)
    vertical_mats = band_matrices(vertical_offsets, basis_width, totals)
    vertical = jnp.einsum(
        "vbij,vjc->vbic", vertical_mats, extended, precision=lax.Precision.HIGHEST
    )
    in_cols = jnp.arange(384)[:, None]
    out_cols = jnp.arange(128)[None, :]
    across_offsets = (in_cols - 128 - out_cols).astype(jnp.float32)
    across_mats = band_matrices(across_offsets, basis_width, totals)
    blocks = col_count // 128
    centre = vertical.reshape(visits_here, BASES, row_count, blocks, 128)
    zero_block = jnp.zeros_like(centre[:, :, :, :1])
    left_side = jnp.concatenate([zero_block, centre[:, :, :, :-1]], axis=3)
    right_side = jnp.concatenate([centre[:, :, :, 1:], zero_block], axis=3)
    stacked = jnp.concatenate([left_side, centre, right_side], axis=4)
    smoothed = jnp.einsum(
        "vbrnk,vbkj->vbrnj", stacked, across_mats, precision=lax.Precision.HIGHEST
    )
    smoothed = smoothed.reshape(visits_here, BASES, row_count, col_count)
    total_rows = row_count * lax.axis_size("tile")
    row_global = (lax.axis_index("tile") * row_count + jnp.arange(row_count)).astype(jnp.float32)
    row_pos = 2.0 * row_global / (total_rows - 1) - 1.0
    col_pos = 2.0 * jnp.arange(col_count).astype(jnp.float32) / (col_count - 1) - 1.0
    ycoord = jnp.broadcast_to(row_pos[:, None], (row_count, col_count))
    xcoord = jnp.broadcast_to(col_pos[None, :], (row_count, col_count))
    poly_terms = jnp.stack(
        [
            jnp.ones((row_count, col_count), jnp.float32),
            xcoord,
            ycoord,
            xcoord * xcoord,
            xcoord * ycoord,
            ycoord * ycoord,
        ]
    )
    factor = jnp.einsum("vbk,krc->vbrc", spatial_coef, poly_terms, precision=lax.Precision.HIGHEST)
    matched = jnp.sum(factor * smoothed, axis=1)
    valid = usable > 0
    low_side = jnp.where(valid, matched, big_value)
    high_side = jnp.where(valid, matched, -big_value)
    big_plane = jnp.full((row_count, col_count), big_value, jnp.float32)
    records = (big_plane, big_plane, big_plane, -big_plane, -big_plane, -big_plane)
    for visit_id in range(visits_here):
        single = (
            low_side[visit_id],
            big_plane,
            big_plane,
            high_side[visit_id],
            -big_plane,
            -big_plane,
        )
        records = merge_records(records, single)
    merged = combined_all(records, "visit", merge_records)
    lower = merged[2]
    upper = merged[5]
    weight = jnp.where(valid, 1.0 / variance, 0.0)
    numer = jnp.sum(weight * jnp.clip(matched, lower, upper), axis=0)
    denom = jnp.sum(weight, axis=0)
    numer_all, denom_all = lax.psum((numer, denom), "visit")
    return numer_all / denom_all


def solution(mesh):
    in_specs = (
        P("visit", ("patch", "tile"), None),
        P("visit", ("patch", "tile"), None),
        P("visit", ("patch", "tile"), None),
        P(("patch", "visit"), None),
        P(("patch", "visit"), None, None),
    )
    out_specs = P(("patch", "tile"), None)
    return jax.shard_map(
        per_device, mesh=mesh, in_specs=in_specs, out_specs=out_specs, check_vma=False
    )
```

profile of v0, /device:TPU:0, one launch (start us, length us, event | category | flops | bytes accessed | tf_op | source)
XLA Modules:
  0.0 457.8 jit_solution(1731907902424152540)
XLA Ops:
  6.5 1.7 fusion.56
  8.3 1.6 copy.46
  9.9 3.3 collective-permute-start
  13.2 1.6 copy.47
  14.8 1.3 collective-permute-start.1
  16.1 0.6 add_convert_fusion
  16.7 0.6 fusion.41
  17.3 0.6 negate_multiply_fusion.1
  17.9 0.1 fusion.31
  18.1 0.1 negate_multiply_fusion
  18.2 0.8 subtract_convert_fusion
  19.0 0.3 slice_reduce_fusion.2
  19.2 0.5 multiply_multiply_fusion.5
  19.8 0.5 multiply_multiply_fusion.3
  20.3 0.5 broadcast_multiply_fusion
  20.8 0.8 fusion.48
  21.6 0.3 stack_broadcast_in_dim.17
  22.0 0.5 stack_broadcast_in_dim.16
  22.5 0.3 stack.11
  22.8 0.5 stack.10
  23.3 0.5 stack_broadcast_in_dim.15
  23.7 8.3 %stack.24 = f32[6,32,4096]{2,0,1:T(8,128)} concatenate(f32[1,32,4096]{2,0,1:T(1,128)S(1)} %stack_broadcast_in_dim.15, f32[1,32,4096]{2,0,1:T(1,128)S(1)} %stack_broadcast_in_dim.16, f32[1,32,4096]{2,0,1:T(1,128)S(1)} %stack_broadcast_in_dim.17, f32[1,32,4096]{2,0,1:T(1,128)S(1)} %stack.10, f32[1,32,4096]{2,0,1:T(1,128)S(1)} %broadcast_multiply_fusion, f32[1,32,4096]{2,0,1:T(1,128)S(1)} %stack.11), dimensions={0} | concatenate | bytes 6291456 | tf_op jit(solution)/shard_map/stack | solution.py:114
  32.1 0.9 fusion.38
  33.0 2.8 fusion.22
  35.8 1.9 copy.35
  37.7 1.8 copy.36
  39.5 5.2 %fusion.9 = f32[4,3,32,4096]{3,2,1,0:T(8,128)S(1)} fusion(f32[4,15,4096]{2,1,0:T(8,128)S(1)} %copy.36, f32[4,32,4096]{2,1,0:T(8,128)S(1)} %copy-done.1, f32[4,15,4096]{2,1,0:T(8,128)S(1)} %copy.35, f32[4,1,32,62]{3,2,1,0:T(8,128)S(1)} %get-tuple-element.382, f32[4,1,32,62]{3,2,1,0:T(8,128)S(1)} %get-tuple-element.381, ...), kind=kOutput, calls=%fused_computation.27 | convolution fusion | flops 1172290048 | bytes 10449920 | tf_op jit(solution)/shard_map/vbij,vjc->vbic/dot_general | solution.py:91
  44.7 1.3 copy.48
  46.0 6.3 %fusion.55 = (f32[4,3,32,31,128]{4,3,2,1,0:T(8,128)}, f32[4,3,32,31,128]{4,3,2,1,0:T(8,128)}) fusion(f32[4,3,32,32,128]{4,3,2,1,0:T(8,128)S(1)} %bitcast.90), kind=kLoop, calls=%fused_computation.139 | loop fusion | bytes 24379392 | tf_op jit(solution)/shard_map/slice | solution.py:101
  52.4 20.0 %fusion.6 = f32[4,3,32,32,128]{4,3,0,1,2:T(8,128)} fusion(f32[4,3,32,31,128]{4,3,2,1,0:T(8,128)} %get-tuple-element.371, f32[4,3,32,31,128]{4,3,2,1,0:T(8,128)} %get-tuple-element.370, f32[4,3,32,32,128]{4,3,2,1,0:T(8,128)S(1)} %bitcast.91, f32[4,1,384,128]{3,2,1,0:T(8,128)} %get-tuple-element.379, f32[4,1,384,128]{3,2,1,0:T(8,128)} %get-tuple-element.378, ...), kind=kOutput, calls=%fused_computation.22 | convolution fusion | flops 7277248512 | bytes 27131904 | tf_op jit(solution)/shard_map/vbrnk,vbkj->vbrnj/dot_general | solution.py:104
  72.4 7.6 %reshape.342 = f32[4,3,32,4096]{3,0,1,2:T(4,128)} reshape(f32[4,3,32,32,128]{4,3,0,1,2:T(8,128)} %fusion.6) | data formatting | bytes 12582912 | tf_op jit(solution)/shard_map/reshape | solution.py:107
  80.0 14.7 %fusion.8 = f32[4,32,4096]{2,0,1:T(4,128)S(1)} fusion(f32[4,3,32,4096]{3,0,1,2:T(4,128)} %reshape.342, f32[6,32,4096]{2,0,1:T(8,128)} %stack.24, f32[4,3,6]{2,0,1:T(4,128)S(1)} %copy-done), kind=kOutput, calls=%fused_computation.25 | convolution fusion | flops 115867648 | bytes 11534624 | tf_op jit(solution)/shard_map/vbk,krc->vbrc/dot_general | solution.py:124
  94.8 1.6 copy_select_fusion
  96.4 1.2 maximum_maximum_fusion
  97.6 1.2 minimum_maximum_fusion
  98.8 0.0 all-gather.13.cloned.1.call-start
  98.9 0.7 all-gather.13.cloned.1.call-update
  99.6 1.5 copy_select_fusion.1
  101.1 1.2 minimum_minimum_fusion
  102.3 1.2 maximum_minimum_fusion
  103.6 0.0 all-gather.7.cloned.1.call-start
  103.6 0.5 all-gather.7.cloned.1.call-update
  104.2 0.5 all-gather.11.cloned.1.call-update
  104.8 0.5 all-gather.17.cloned.1.call-update
  105.3 0.0 all-reduce.5.cloned.1.call-start
  105.4 43.2 %all-gather.15.cloned.1.call-done = f32[4,32,4096]{2,1,0:T(8,128)} async-done(((f32[1,32,4096]{2,1,0:T(8,128)}), f32[4,32,4096]{2,1,0:T(8,128)}) %all-gather.15.cloned.1.call-update) | async-done | bytes 2097168 | tf_op jit(solution)/shard_map/all_gather | solution.py:31
  148.6 1.9 slice_bitcast_fusion.1
  150.4 44.4 %all-gather.13.cloned.1.call-done = f32[4,32,4096]{2,1,0:T(8,128)} async-done(((f32[1,32,4096]{2,1,0:T(8,128)}), f32[4,32,4096]{2,1,0:T(8,128)}) %all-gather.13.cloned.1.call-update) | async-done | bytes 2097168 | tf_op jit(solution)/shard_map/all_gather | solution.py:31
  194.8 1.8 slice_bitcast_fusion.2
  196.7 44.4 %all-gather.9.cloned.1.call-done = f32[4,32,4096]{2,1,0:T(8,128)} async-done(((f32[1,32,4096]{2,1,0:T(8,128)}), f32[4,32,4096]{2,1,0:T(8,128)}) %all-gather.9.cloned.1.call-update) | async-done | bytes 2097168 | tf_op jit(solution)/shard_map/all_gather | solution.py:31
  241.1 1.9 slice_bitcast_fusion.4
  243.0 44.2 %all-gather.7.cloned.1.call-done = f32[4,32,4096]{2,1,0:T(8,128)} async-done(((f32[1,32,4096]{2,1,0:T(8,128)}), f32[4,32,4096]{2,1,0:T(8,128)}) %all-gather.7.cloned.1.call-update) | async-done | bytes 2097168 | tf_op jit(solution)/shard_map/all_gather | solution.py:31
  287.2 1.9 slice_bitcast_fusion.5
  289.1 44.2 %all-gather.11.cloned.1.call-done = f32[4,32,4096]{2,1,0:T(8,128)} async-done(((f32[1,32,4096]{2,1,0:T(8,128)}), f32[4,32,4096]{2,1,0:T(8,128)}) %all-gather.11.cloned.1.call-update) | async-done | bytes 2097168 | tf_op jit(solution)/shard_map/all_gather | solution.py:31
  333.3 1.1 slice_bitcast_fusion.3
  334.4 45.0 %all-gather.17.cloned.1.call-done = f32[4,32,4096]{2,1,0:T(8,128)} async-done(((f32[1,32,4096]{2,1,0:T(8,128)}), f32[4,32,4096]{2,1,0:T(8,128)}) %all-gather.17.cloned.1.call-update) | async-done | bytes 2097168 | tf_op jit(solution)/shard_map/all_gather | solution.py:31
  379.4 1.1 slice_bitcast_fusion
  380.5 12.9 %while.25 = (s32[]{:T(128)}, f32[32,4096]{1,0:T(8,128)}, f32[32,4096]{1,0:T(8,128)}, f32[32,4096]{1,0:T(8,128)S(1)}, f32[32,4096]{1,0:T(8,128)}, /*index=5*/f32[...) while((s32[]{:T(128)}, f32[32,4096]{1,0:T(8,128)}, ...), condition=%wide.region_5.6_spmd, body=%wide.region_4.5_spmd.sunk | while | flops 2359301 | bytes 9437379 | solution.py:37
  380.5 4.3 fusion.58
  384.8 4.3 fusion.58
  389.1 4.3 fusion.58
  393.4 4.5 fusion.25
  397.9 51.1 %all-reduce.5.cloned.1.call-done = (f32[32,4096]{1,0:T(8,128)}, f32[32,4096]{1,0:T(8,128)}) async-done(((f32[32,4096]{1,0:T(8,128)}, f32[32,4096]{1,0:T(8,128)}), (f32[32,4096]{1,0:T(8,128)}, f32[32,4096]{1,0:T(8,128)})) %all-reduce.5.cloned.1.call-update) | async-done | bytes 1048592 | tf_op jit(solution)/shard_map/psum | solution.py:147
  448.9 2.1 div.443
  (25 shorter events, 0.2 us)
Async XLA Ops:
  6.5 73.5 %copy-start = (f32[4,3,6]{2,0,1:T(4,128)S(1)}, f32[4,3,6]{2,0,1:T(4,128)}, u32[]{:S(2)}) copy-start(f32[4,3,6]{2,0,1:T(4,128)} %param.11) | copy-start | bytes 868
  6.5 142.0 %all-gather.15.cloned.1.call-start = ((), (), s32[]{:S(2)}) async-start(), calls=%async_computation.4 | async-start | bytes 2621440 | tf_op jit(solution)/shard_map/all_gather | solution.py:31
  8.3 10.7 %copy-start.4 = (f32[4,3]{1,0:T(4,128)S(1)}, f32[4,3]{1,0:T(4,128)}, u32[]{:S(2)}) copy-start(f32[4,3]{1,0:T(4,128)} %param.10) | copy-start | bytes 148
  9.9 25.9 %collective-permute-start = (f32[4,15,4096]{2,0,1:T(4,128)}, f32[4,15,4096]{2,0,1:T(4,128)}, u32[]{:S(2)}, u32[]{:S(2)}) collective-permute-start(f32[4,15,4096]{2,0,1:T(4,128)} %copy.46), channel_id=1, source_target_pairs={{0,1},{1,2},{2,3},{4,5},{5,6},{6,7},{8,9},{9,10},{10,11},{12,13},{... | collective-permute-start | bytes 2949128 | tf_op jit(solution)/shard_map/ppermute | solution.py:21
  14.8 22.9 %collective-permute-start.1 = (f32[4,15,4096]{2,0,1:T(4,128)}, f32[4,15,4096]{2,0,1:T(4,128)}, u32[]{:S(2)}, u32[]{:S(2)}) collective-permute-start(f32[4,15,4096]{2,0,1:T(4,128)} %copy.47), channel_id=1, source_target_pairs={{1,0},{2,1},{3,2},{5,4},{6,5},{7,6},{9,8},{10,9},{11,10},{13,12},{... | collective-permute-start | bytes 2949128 | tf_op jit(solution)/shard_map/ppermute | solution.py:23
  35.8 3.7 copy-start.1
  80.0 14.8 %copy-start.3 = (s32[4,32,4096]{2,1,0:T(8,128)S(1)}, s32[4,32,4096]{2,1,0:T(8,128)}, u32[]{:S(2)}) copy-start(s32[4,32,4096]{2,1,0:T(8,128)} %param.9) | copy-start | bytes 6291460
  96.4 3.3 copy-start.2
  98.8 96.0 %all-gather.13.cloned.1.call-start = ((), (), s32[]{:S(2)}) async-start(), calls=%async_computation.3 | async-start | bytes 2621440 | tf_op jit(solution)/shard_map/all_gather | solution.py:31
  99.6 141.5 %all-gather.9.cloned.1.call-start = ((), (), s32[]{:S(2)}) async-start(), calls=%async_computation.1 | async-start | bytes 2621440 | tf_op jit(solution)/shard_map/all_gather | solution.py:31
  103.6 183.6 %all-gather.7.cloned.1.call-start = ((), (), s32[]{:S(2)}) async-start(), calls=%async_computation | async-start | bytes 2621440 | tf_op jit(solution)/shard_map/all_gather | solution.py:31
  104.2 229.2 %all-gather.11.cloned.1.call-start = ((), (), s32[]{:S(2)}) async-start(), calls=%async_computation.2 | async-start | bytes 2621440 | tf_op jit(solution)/shard_map/all_gather | solution.py:31
  104.7 274.7 %all-gather.17.cloned.1.call-start = ((), (), s32[]{:S(2)}) async-start(), calls=%async_computation.5 | async-start | bytes 2621440 | tf_op jit(solution)/shard_map/all_gather | solution.py:31
  105.3 343.6 %all-reduce.5.cloned.1.call-start = ((), (), s32[]{:S(2)}) async-start(), calls=%async_computation.6 | async-start | bytes 2097152 | tf_op jit(solution)/shard_map/psum | solution.py:147
Sparse Core Ops, SparseCore 0:
  99.0 49.5 all-gather.14
  150.1 44.6 all-gather.12
  196.4 44.6 all-gather.8
  242.5 44.6 all-gather.6
  288.6 44.6 all-gather.10
  334.7 44.6 all-gather.16
  398.0 50.8 all-reduce.4
where the time goes:
time: 459 us; the launch traced here: 458 us
  waiting for transfers between devices  319 us (69%)
  local copies, waits for them, and re-layouts  43.9 us (10%)
  matrix products  40 us (9%)
  other arithmetic  36.5 us (8%)
  between operations  13.7 us (3%)
  starting transfers between devices  4.83 us (1%)
    all_gather x6, waiting for transfers between devices, combined_all(): everything = jax.tree.map(lambda part: lax.all_gather(part, axis), array)  265 us
    psum x1, waiting for transfers between devices, per_device(): numer_all, denom_all = lax.psum((numer, denom), 'visit')  51.1 us
    dot_general x1, matrix products, per_device(): jnp.einsum('vbrnk,vbkj->vbrnj', stacked, across_mats, precision=lax.Preci...  20 us
    dot_general x1, matrix products, per_device(): jnp.einsum('vbk,krc->vbrc', spatial_coef, poly_terms, precision=lax.Preci...  14.7 us
    max x4, other arithmetic, merge_records(): jnp.maximum(jnp.maximum(first[5], second[5]), jnp.maximum(jnp.minimum(fir...  14.1 us
    another operation x6, local copies, waits for them, and re-layouts, per_device(): jnp.stack([jnp.ones((row_count, col_count), jnp.float32), xcoord, ycoord,...  10.4 us
    squeeze x6, local copies, waits for them, and re-layouts, combined_all(): initial = jax.tree.map(lambda part: part[0], everything)  9.62 us
  transfers between devices with their start and end apart: 9, of which 7 were waited for; matrix products, arithmetic and copies ran while one was open for 8% of the time, Pallas kernels for 0%

commit v1 on v0

v1 whole, which is shorter than its diff:
```python
import functools

import jax
import jax.numpy as jnp
from jax import lax
from jax.experimental import pallas as pl
from jax.experimental.pallas import tpu as pltpu
from jax.sharding import PartitionSpec as P

KHALF = 15
BASES = 3
TERMS = 6
HALO = 16
BLOCK = 256
SIDE = 128
SCALARS = 2 + TERMS
MESH = pl.DeviceIdType.MESH

big_value = 1e30


def band(offsets, narrow, norm, basis_id):
    square = (offsets * offsets).astype(jnp.float32)
    profile = jnp.exp(-square * narrow) * norm
    for _ in range(basis_id):
        profile = profile * (square * (2.0 * narrow))
    return jnp.where(jnp.abs(offsets) <= KHALF, profile, 0.0)


def split(values):
    high = values.astype(jnp.bfloat16)
    low = (values - high.astype(jnp.float32)).astype(jnp.bfloat16)
    return high, low


def dot(a, b):
    return jnp.dot(a, b, preferred_element_type=jnp.float32)


def kernel(
    tiles, owners,
    scal_ref, expo_ref, var_ref, use_ref, out_ref,
    halo, w_own, m_own, w_got, m_got, vert_hi, vert_lo, total, result,
    halo_send, halo_got, w_send, w_recv, m_send, m_recv, r_send, r_recv,
):
    visits, rows, cols = expo_ref.shape
    blocks = cols // BLOCK
    mine_blocks = blocks // owners
    share = mine_blocks * rows
    me = lax.axis_index("visit")
    tile = lax.axis_index("tile")
    has_up = tile > 0
    has_down = tile < tiles - 1
    peers = [lax.rem(me + d, owners) for d in range(1, owners)]

    barrier = pltpu.get_barrier_semaphore()
    for peer in peers:
        pl.semaphore_signal(barrier, inc=1, device_id={"visit": peer}, device_id_type=MESH)

    @pl.when(has_up)
    def _():
        pl.semaphore_signal(barrier, inc=1, device_id={"tile": tile - 1}, device_id_type=MESH)

    @pl.when(has_down)
    def _():
        pl.semaphore_signal(barrier, inc=1, device_id={"tile": tile + 1}, device_id_type=MESH)

    beside = has_up.astype(jnp.int32) + has_down.astype(jnp.int32)
    pl.semaphore_wait(barrier, owners - 1 + beside)

    def halo_copy(side, v):
        start = rows - HALO if side == 0 else 0
        return pltpu.make_async_remote_copy(
            src_ref=expo_ref.at[v, pl.ds(start, HALO), :],
            dst_ref=halo.at[side, v],
            send_sem=halo_send.at[side, v],
            recv_sem=halo_got.at[side, v],
            device_id={"tile": tile + 1 if side == 0 else tile - 1},
            device_id_type=MESH,
        )

    @pl.when(has_down)
    def _():
        for v in range(visits):
            halo_copy(0, v).start()

    @pl.when(has_up)
    def _():
        for v in range(visits):
            halo_copy(1, v).start()

    @pl.when(jnp.logical_not(has_up))
    def _():
        halo[0] = jnp.zeros(halo.shape[1:], jnp.float32)

    @pl.when(jnp.logical_not(has_down))
    def _():
        halo[1] = jnp.zeros(halo.shape[1:], jnp.float32)

    def w_copy(peer, k):
        return pltpu.make_async_remote_copy(
            src_ref=w_own.at[peer], dst_ref=w_got.at[me],
            send_sem=w_send.at[k], recv_sem=w_recv.at[me],
            device_id={"visit": peer}, device_id_type=MESH,
        )

    def m_copy(peer, k, v):
        return pltpu.make_async_remote_copy(
            src_ref=m_own.at[peer, v], dst_ref=m_got.at[me, v],
            send_sem=m_send.at[k, v], recv_sem=m_recv.at[me, v],
            device_id={"visit": peer}, device_id_type=MESH,
        )

    def r_copy(peer, k):
        return pltpu.make_async_remote_copy(
            src_ref=result.at[me], dst_ref=result.at[me],
            send_sem=r_send.at[k], recv_sem=r_recv.at[me],
            device_id={"visit": peer}, device_id_type=MESH,
        )

    def weights_for(owner):
        def step(v, carry):
            for j in range(mine_blocks):
                first = pl.multiple_of((owner * mine_blocks + j) * BLOCK, BLOCK)
                there = pl.ds(first, BLOCK)
                w_own[owner, v, pl.ds(j * rows, rows), :] = jnp.where(
                    use_ref[v, :, there] > 0, 1.0 / var_ref[v, :, there], 0.0
                )
            return carry

        lax.fori_loop(0, visits, step, 0)

    for k, peer in enumerate(peers):
        weights_for(peer)
        w_copy(peer, k).start()
    weights_for(me)

    wide = cols + 2 * SIDE
    for ref in (vert_hi, vert_lo):
        ref[:, pl.ds(0, SIDE)] = jnp.zeros((BASES * rows, SIDE), jnp.bfloat16)
        ref[:, pl.ds(wide - SIDE, SIDE)] = jnp.zeros((BASES * rows, SIDE), jnp.bfloat16)

    reach = rows + 2 * HALO
    depth = BLOCK + 2 * SIDE
    stacked = blocks * rows

    def visit_step(v, carry):
        @pl.when(has_up)
        def _():
            halo_copy(0, v).wait_recv()

        @pl.when(has_down)
        def _():
            halo_copy(1, v).wait_recv()

        out_row = lax.broadcasted_iota(jnp.int32, (rows, 3 * reach), 0)
        in_row = lax.broadcasted_iota(jnp.int32, (rows, 3 * reach), 1)
        third = in_row >= 2 * reach
        in_row = jnp.where(third, in_row - 2 * reach, jnp.where(in_row >= reach, in_row - reach, in_row))
        pieces = []
        for b in range(BASES):
            mat = band(in_row - HALO - out_row, scal_ref[v, b * SCALARS], scal_ref[v, b * SCALARS + 1], b)
            high = mat.astype(jnp.bfloat16).astype(jnp.float32)
            pieces.append(jnp.where(third, mat - high, high))
        down = jnp.concatenate(pieces, axis=0).astype(jnp.bfloat16)

        def column_step(n, inner):
            there = pl.ds(pl.multiple_of(n * 2 * BLOCK, 2 * BLOCK), 2 * BLOCK)
            image = jnp.concatenate([halo[0, v, :, there], expo_ref[v, :, there], halo[1, v, :, there]], axis=0)
            high, low = split(image)
            vert = dot(down, jnp.concatenate([high, low, high], axis=0))
            high, low = split(vert)
            here = pl.ds(pl.multiple_of(n * 2 * BLOCK + SIDE, SIDE), 2 * BLOCK)
            vert_hi[:, here] = high
            vert_lo[:, here] = low
            return inner

        lax.fori_loop(0, blocks // 2, column_step, 0)

        in_col = lax.broadcasted_iota(jnp.int32, (depth, BLOCK), 0)
        out_col = lax.broadcasted_iota(jnp.int32, (depth, BLOCK), 1)
        for b in range(BASES):
            narrow, norm = scal_ref[v, b * SCALARS], scal_ref[v, b * SCALARS + 1]
            across_hi, across_lo = split(band(in_col - SIDE - out_col, narrow, norm, b))
            c = [scal_ref[v, b * SCALARS + 2 + k] for k in range(TERMS)]
            for d in range(owners):
                left = [
                    jnp.concatenate(
                        [
                            ref[pl.ds(b * rows, rows), pl.ds((d * mine_blocks + j) * BLOCK, depth)]
                            for j in range(mine_blocks)
                        ],
                        axis=0,
                    )
                    for ref in (vert_hi, vert_lo)
                ]
                smooth = dot(left[0], across_hi) + dot(left[1], across_hi) + dot(left[0], across_lo)
                row = lax.broadcasted_iota(jnp.int32, (share, BLOCK), 0)
                col = lax.broadcasted_iota(jnp.int32, (share, BLOCK), 1)
                col = col + (d * mine_blocks + row // rows) * BLOCK
                row = row % rows + tile * rows
                y = row.astype(jnp.float32) * (2.0 / (tiles * rows - 1)) - 1.0
                x = col.astype(jnp.float32) * (2.0 / (cols - 1)) - 1.0
                factor = (c[0] + y * (c[2] + y * c[5])) + x * (c[1] + y * c[4] + x * c[3])
                term = factor * smooth
                here = pl.ds(d * share, share)
                if b == 0:
                    total[here, :] = term
                elif b < BASES - 1:
                    total[here, :] += term
                else:
                    m_own[d, v] = total[here, :] + term
        for k, peer in enumerate(peers):
            m_copy(peer, k, v).start()
        return carry

    lax.fori_loop(0, visits, visit_step, 0)

    def got_w(s):
        return pltpu.make_async_remote_copy(
            src_ref=w_own.at[s], dst_ref=w_got.at[s], send_sem=w_send.at[0], recv_sem=w_recv.at[s],
            device_id={"visit": s}, device_id_type=MESH,
        )

    def got_m(s, v):
        return pltpu.make_async_remote_copy(
            src_ref=m_own.at[s, v], dst_ref=m_got.at[s, v], send_sem=m_send.at[0, v], recv_sem=m_recv.at[s, v],
            device_id={"visit": s}, device_id_type=MESH,
        )

    def got_r(s):
        return pltpu.make_async_remote_copy(
            src_ref=result.at[s], dst_ref=result.at[s], send_sem=r_send.at[0], recv_sem=r_recv.at[s],
            device_id={"visit": s}, device_id_type=MESH,
        )

    for peer in peers:
        got_w(peer).wait_recv()
        for v in range(visits):
            got_m(peer, v).wait_recv()

    sources = [(m_own, w_own, me)] + [(m_got, w_got, peer) for peer in peers]
    strip = 16

    def strip_step(i, carry):
        here = pl.ds(pl.multiple_of(i * strip, strip), strip)
        full = jnp.full((strip, BLOCK), big_value, jnp.float32)
        l1 = l2 = l3 = full
        h1 = h2 = h3 = -full
        for m_ref, w_ref, s in sources:
            for v in range(visits):
                m = m_ref[s, v, here, :]
                valid = w_ref[s, v, here, :] > 0.0
                low = jnp.where(valid, m, big_value)
                high = jnp.where(valid, m, -big_value)
                l3 = jnp.minimum(l3, jnp.maximum(l2, low))
                l2 = jnp.minimum(l2, jnp.maximum(l1, low))
                l1 = jnp.minimum(l1, low)
                h3 = jnp.maximum(h3, jnp.minimum(h2, high))
                h2 = jnp.maximum(h2, jnp.minimum(h1, high))
                h1 = jnp.maximum(h1, high)
        numer = jnp.zeros((strip, BLOCK), jnp.float32)
        denom = numer
        for m_ref, w_ref, s in sources:
            for v in range(visits):
                w = w_ref[s, v, here, :]
                m = jnp.minimum(jnp.maximum(m_ref[s, v, here, :], l3), h3)
                numer = numer + w * m
                denom = denom + w
        result[me, here, :] = numer / denom
        return carry

    lax.fori_loop(0, share // strip, strip_step, 0)
    for k, peer in enumerate(peers):
        r_copy(peer, k).start()
    for peer in peers:
        got_r(peer).wait_recv()
    for s in range(owners):
        for j in range(mine_blocks):
            out_ref[:, pl.ds((s * mine_blocks + j) * BLOCK, BLOCK)] = result[s, pl.ds(j * rows, rows), :]

    for k, peer in enumerate(peers):
        w_copy(peer, k).wait_send()
        for v in range(visits):
            m_copy(peer, k, v).wait_send()
        r_copy(peer, k).wait_send()

    @pl.when(has_down)
    def _():
        for v in range(visits):
            halo_copy(0, v).wait_send()

    @pl.when(has_up)
    def _():
        for v in range(visits):
            halo_copy(1, v).wait_send()


def per_device(exposure, variance, usable, basis_width, spatial_coef):
    visits, rows, cols = exposure.shape
    tiles, owners = lax.axis_size("tile"), lax.axis_size("visit")
    share = cols // BLOCK // owners * rows
    narrow = 0.5 / (basis_width * basis_width)
    offsets = jnp.arange(-KHALF, KHALF + 1).astype(jnp.float32)
    square = (offsets * offsets)[None, None, :]
    powers = [jnp.ones_like(square), square, square * square]
    raw = jnp.exp(-square * narrow[:, :, None]) * jnp.stack(
        [powers[b][:, 0] * ((2.0 * narrow[:, b]) ** b)[:, None] for b in range(BASES)], axis=1
    )
    norm = 1.0 / jnp.sum(raw, axis=2)
    scalars = jnp.concatenate([narrow[:, :, None], norm[:, :, None], spatial_coef], axis=2)
    scalars = scalars.reshape(visits, BASES * SCALARS)
    f32, dma = jnp.float32, pltpu.SemaphoreType.DMA
    vmem = pl.BlockSpec(memory_space=pltpu.VMEM)
    return pl.pallas_call(
        functools.partial(kernel, tiles, owners),
        out_shape=jax.ShapeDtypeStruct((rows, cols), f32),
        in_specs=[pl.BlockSpec(memory_space=pltpu.SMEM), vmem, vmem, vmem],
        out_specs=vmem,
        scratch_shapes=[
            pltpu.VMEM((2, visits, HALO, cols), f32),
            pltpu.VMEM((owners, visits, share, BLOCK), f32),
            pltpu.VMEM((owners, visits, share, BLOCK), f32),
            pltpu.VMEM((owners, visits, share, BLOCK), f32),
            pltpu.VMEM((owners, visits, share, BLOCK), f32),
            pltpu.VMEM((BASES * rows, cols + 2 * SIDE), jnp.bfloat16),
            pltpu.VMEM((BASES * rows, cols + 2 * SIDE), jnp.bfloat16),
            pltpu.VMEM((owners * share, BLOCK), f32),
            pltpu.VMEM((owners, share, BLOCK), f32),
            dma((2, visits)),
            dma((2, visits)),
            dma((owners,)),
            dma((owners,)),
            dma((owners, visits)),
            dma((owners, visits)),
            dma((owners,)),
            dma((owners,)),
        ],
        compiler_params=pltpu.CompilerParams(
            collective_id=0, has_side_effects=True, vmem_limit_bytes=48 * 1024 * 1024
        ),
    )(scalars, exposure, variance, usable)


def solution(mesh):
    in_specs = (
        P("visit", ("patch", "tile"), None),
        P("visit", ("patch", "tile"), None),
        P("visit", ("patch", "tile"), None),
        P(("patch", "visit"), None),
        P(("patch", "visit"), None, None),
    )
    out_specs = P(("patch", "tile"), None)
    return jax.shard_map(
        per_device, mesh=mesh, in_specs=in_specs, out_specs=out_specs, check_vma=False
    )
```

time: 459 us -> 117 us (0.25)
  waiting for transfers between devices: 319 us -> 0 us
  Pallas kernels: 0 us -> 109 us
  matrix products: 40 us -> 0 us
  local copies, waits for them, and re-layouts: 43.9 us -> 4.38 us
  other arithmetic: 36.5 us -> 2.64 us
  between operations: 13.7 us -> 0.02 us
  starting transfers between devices: 4.83 us -> 0 us
    all_gather x6 -> x0, waiting for transfers between devices: 265 us -> none  [combined_all(): everything = jax.tree.map(lambda part: lax.all_gather(part, axis), array)]
    pallas_call x0 -> x1, Pallas kernels: none -> 109 us  [per_device(): pl.pallas_call(functools.partial(kernel, tiles, owners), out_shape=jax.Sh...]
    psum x1 -> x0, waiting for transfers between devices: 51.1 us -> none  [per_device(): numer_all, denom_all = lax.psum((numer, denom), 'visit')]
    dot_general x3 -> x0, matrix products: 40 us -> none  [the longest x1 20 us: per_device(): jnp.einsum('vbrnk,vbkj->vbrnj', stacked, across_mats, precision=lax.Preci...]
    max x5 -> x0, other arithmetic: 15.3 us -> none  [the longest x4 14.1 us: merge_records(): jnp.maximum(jnp.maximum(first[5], second[5]), jnp.maximum(jnp.minimum(fir...]
    another operation x6 -> x1, local copies, waits for them, and re-layouts: 10.4 us -> 0.01 us  [per_device(): jnp.stack([powers[b][:, 0] * ((2.0 * narrow[:, b]) ** b)[:, None] for b i...]
    squeeze x6 -> x0, local copies, waits for them, and re-layouts: 9.62 us -> none  [combined_all(): initial = jax.tree.map(lambda part: part[0], everything)]
    slice x2 -> x0, local copies, waits for them, and re-layouts: 8.05 us -> none  [the longest x1 6.31 us: per_device(): left_side = jnp.concatenate([zero_block, centre[:, :, :, :-1]], axis=3)]
  transfers between devices with their start and end apart: 9 -> 0, of which waited for: 7 -> 0; matrix products, arithmetic and copies ran while one was open for 8% -> 0% of each run, Pallas kernels for 0% -> 0%
where the time goes in v1:
time: 117 us; the launch traced here: 116 us
  Pallas kernels  109 us (93%)
  local copies, waits for them, and re-layouts  4.38 us (4%)
  other arithmetic  2.64 us (2%)
    pallas_call x1, Pallas kernels, per_device(): pl.pallas_call(functools.partial(kernel, tiles, owners), out_shape=jax.Sh...  109 us
    unnamed x5, local copies, waits for them, and re-layouts  3.98 us

profile of v1, /device:TPU:0, one launch (start us, length us, event | category | flops | bytes accessed | tf_op | source)
XLA Modules:
  0.0 115.9 jit_solution(10876318049867093836)
XLA Ops:
  0.0 0.7 multiply_divide_fusion
  0.7 0.2 multiply_reduce_fusion.1
  0.9 0.1 copy.12
  1.0 0.7 fusion.3
  1.7 0.1 broadcast_multiply_fusion
  1.8 0.2 fusion
  2.0 0.1 copy.15
  2.1 0.1 copy.14
  2.2 0.8 pad_maximum_fusion
  3.0 0.1 reshape.122.scal_ref
  3.1 0.0 copy-start
  3.1 1.6 %copy-done = f32[4,32,4096]{2,1,0:T(8,128)S(1)} copy-done((f32[4,32,4096]{2,1,0:T(8,128)S(1)}, f32[4,32,4096]{2,1,0:T(8,128)}, u32[]{:S(2)}) %copy-start) | copy-done | bytes 2097176
  4.7 0.0 copy-start.1
  4.7 1.6 %copy-done.1 = f32[4,32,4096]{2,1,0:T(8,128)S(1)} copy-done((f32[4,32,4096]{2,1,0:T(8,128)S(1)}, f32[4,32,4096]{2,1,0:T(8,128)}, u32[]{:S(2)}) %copy-start.1) | copy-done | bytes 2097176
  6.2 108.8 %shard_map.55 = f32[32,4096]{1,0:T(8,128)S(1)} custom-call(f32[4,24]{1,0:T(4,128)S(1)} %reshape.122.scal_ref, f32[4,32,4096]{2,1,0:T(8,128)S(1)} %copy-done, f32[4,32,4096]{2,1,0:T(8,128)S(1)} %copy-done.1, s32[4,32,4096]{2,1,0:T(8,128)} %use_ref.1), custom_call_target="tpu_custom_call" | custom-call | tf_op jit(solution)/shard_map/pallas_call | solution.py:315
  115.1 0.8 copy.20
  (6 shorter events, 0.0 us)
Async XLA Ops:
  3.1 1.6 %copy-start = (f32[4,32,4096]{2,1,0:T(8,128)S(1)}, f32[4,32,4096]{2,1,0:T(8,128)}, u32[]{:S(2)}) copy-start(f32[4,32,4096]{2,1,0:T(8,128)} %expo_ref.1) | copy-start | bytes 6291460
  4.7 1.6 %copy-start.1 = (f32[4,32,4096]{2,1,0:T(8,128)S(1)}, f32[4,32,4096]{2,1,0:T(8,128)}, u32[]{:S(2)}) copy-start(f32[4,32,4096]{2,1,0:T(8,128)} %var_ref.1) | copy-start | bytes 6291460

commit v2 on v1

--- a/solution.py
+++ b/solution.py
@@ -13,7 +13,7 @@
 HALO = 16
 BLOCK = 256
 SIDE = 128
-SCALARS = 2 + TERMS
+HALVES = 2
 MESH = pl.DeviceIdType.MESH
 
 big_value = 1e30
@@ -39,9 +39,9 @@
 
 def kernel(
     tiles, owners,
-    scal_ref, expo_ref, var_ref, use_ref, out_ref,
-    halo, w_own, m_own, w_got, m_got, vert_hi, vert_lo, total, result,
-    halo_send, halo_got, w_send, w_recv, m_send, m_recv, r_send, r_recv,
+    width_ref, coef_ref, expo_hbm, var_hbm, use_hbm, out_ref,
+    expo_ref, var_ref, use_ref, halo, w_own, m_own, w_got, m_got, vert_hi, vert_lo, total, result,
+    expo_sem, var_sem, use_sem, halo_send, halo_got, w_send, w_recv, m_send, m_recv, r_send, r_recv,
 ):
     visits, rows, cols = expo_ref.shape
     blocks = cols // BLOCK
@@ -51,7 +51,14 @@
     tile = lax.axis_index("tile")
     has_up = tile > 0
     has_down = tile < tiles - 1
-    peers = [lax.rem(me + d, owners) for d in range(1, owners)]
+    far_first = sorted(range(1, owners), key=lambda d: (abs(2 * d - owners), d))
+    peers = [lax.rem(me + d, owners) for d in far_first]
+    load_var = pltpu.make_async_copy(var_hbm, var_ref, var_sem)
+    load_use = pltpu.make_async_copy(use_hbm, use_ref, use_sem)
+    load_expo = pltpu.make_async_copy(expo_hbm, expo_ref, expo_sem)
+    load_var.start()
+    load_use.start()
+    load_expo.start()
 
     barrier = pltpu.get_barrier_semaphore()
     for peer in peers:
@@ -71,7 +78,7 @@
     def halo_copy(side, v):
         start = rows - HALO if side == 0 else 0
         return pltpu.make_async_remote_copy(
-            src_ref=expo_ref.at[v, pl.ds(start, HALO), :],
+            src_ref=expo_hbm.at[v, pl.ds(start, HALO), :],
             dst_ref=halo.at[side, v],
             send_sem=halo_send.at[side, v],
             recv_sem=halo_got.at[side, v],
@@ -104,17 +111,19 @@
             device_id={"visit": peer}, device_id_type=MESH,
         )
 
-    def m_copy(peer, k, v):
-        return pltpu.make_async_remote_copy(
-            src_ref=m_own.at[peer, v], dst_ref=m_got.at[me, v],
-            send_sem=m_send.at[k, v], recv_sem=m_recv.at[me, v],
+    half = share // HALVES
+
+    def m_copy(peer, k, v, h):
+        return pltpu.make_async_remote_copy(
+            src_ref=m_own.at[peer, v, pl.ds(h * half, half)], dst_ref=m_got.at[me, v, pl.ds(h * half, half)],
+            send_sem=m_send.at[k, v, h], recv_sem=m_recv.at[me, v, h],
             device_id={"visit": peer}, device_id_type=MESH,
         )
 
-    def r_copy(peer, k):
-        return pltpu.make_async_remote_copy(
-            src_ref=result.at[me], dst_ref=result.at[me],
-            send_sem=r_send.at[k], recv_sem=r_recv.at[me],
+    def r_copy(peer, k, h):
+        return pltpu.make_async_remote_copy(
+            src_ref=result.at[me, pl.ds(h * half, half)], dst_ref=result.at[me, pl.ds(h * half, half)],
+            send_sem=r_send.at[k, h], recv_sem=r_recv.at[me, h],
             device_id={"visit": peer}, device_id_type=MESH,
         )
 
@@ -130,10 +139,13 @@
 
         lax.fori_loop(0, visits, step, 0)
 
+    load_var.wait()
+    load_use.wait()
     for k, peer in enumerate(peers):
         weights_for(peer)
         w_copy(peer, k).start()
     weights_for(me)
+    load_expo.wait()
 
     wide = cols + 2 * SIDE
     for ref in (vert_hi, vert_lo):
@@ -152,6 +164,14 @@
         @pl.when(has_down)
         def _():
             halo_copy(1, v).wait_recv()
+
+        lane = lax.broadcasted_iota(jnp.int32, (8, 2 * SIDE), 1)
+        scales = []
+        for b in range(BASES):
+            width = jnp.full((1, 1), width_ref[v, b], jnp.float32)
+            narrow = 0.5 / (width * width)
+            whole = jnp.sum(band(lane - SIDE, narrow, 1.0, b), axis=1, keepdims=True)
+            scales.append((narrow, 1.0 / whole[0:1]))
 
         out_row = lax.broadcasted_iota(jnp.int32, (rows, 3 * reach), 0)
         in_row = lax.broadcasted_iota(jnp.int32, (rows, 3 * reach), 1)
@@ -159,7 +179,7 @@
         in_row = jnp.where(third, in_row - 2 * reach, jnp.where(in_row >= reach, in_row - reach, in_row))
         pieces = []
         for b in range(BASES):
-            mat = band(in_row - HALO - out_row, scal_ref[v, b * SCALARS], scal_ref[v, b * SCALARS + 1], b)
+            mat = band(in_row - HALO - out_row, *scales[b], b)
             high = mat.astype(jnp.bfloat16).astype(jnp.float32)
             pieces.append(jnp.where(third, mat - high, high))
         down = jnp.concatenate(pieces, axis=0).astype(jnp.bfloat16)
@@ -180,9 +200,8 @@
         in_col = lax.broadcasted_iota(jnp.int32, (depth, BLOCK), 0)
         out_col = lax.broadcasted_iota(jnp.int32, (depth, BLOCK), 1)
         for b in range(BASES):
-            narrow, norm = scal_ref[v, b * SCALARS], scal_ref[v, b * SCALARS + 1]
-            across_hi, across_lo = split(band(in_col - SIDE - out_col, narrow, norm, b))
-            c = [scal_ref[v, b * SCALARS + 2 + k] for k in range(TERMS)]
+            across_hi, across_lo = split(band(in_col - SIDE - out_col, *scales[b], b))
+            c = [coef_ref[v, b, k] for k in range(TERMS)]
             for d in range(owners):
                 left = [
                     jnp.concatenate(
@@ -210,8 +229,9 @@
                     total[here, :] += term
                 else:
                     m_own[d, v] = total[here, :] + term
-        for k, peer in enumerate(peers):
-            m_copy(peer, k, v).start()
+        for h in range(HALVES):
+            for k, peer in enumerate(peers):
+                m_copy(peer, k, v, h).start()
         return carry
 
     lax.fori_loop(0, visits, visit_step, 0)
@@ -222,22 +242,24 @@
             device_id={"visit": s}, device_id_type=MESH,
         )
 
-    def got_m(s, v):
-        return pltpu.make_async_remote_copy(
-            src_ref=m_own.at[s, v], dst_ref=m_got.at[s, v], send_sem=m_send.at[0, v], recv_sem=m_recv.at[s, v],
+    def got_m(s, v, h):
+        there = pl.ds(h * half, half)
+        return pltpu.make_async_remote_copy(
+            src_ref=m_own.at[s, v, there], dst_ref=m_got.at[s, v, there],
+            send_sem=m_send.at[0, v, h], recv_sem=m_recv.at[s, v, h],
             device_id={"visit": s}, device_id_type=MESH,
         )
 
-    def got_r(s):
-        return pltpu.make_async_remote_copy(
-            src_ref=result.at[s], dst_ref=result.at[s], send_sem=r_send.at[0], recv_sem=r_recv.at[s],
+    def got_r(s, h):
+        there = pl.ds(h * half, half)
+        return pltpu.make_async_remote_copy(
+            src_ref=result.at[s, there], dst_ref=result.at[s, there],
+            send_sem=r_send.at[0, h], recv_sem=r_recv.at[s, h],
             device_id={"visit": s}, device_id_type=MESH,
         )
 
     for peer in peers:
         got_w(peer).wait_recv()
-        for v in range(visits):
-            got_m(peer, v).wait_recv()
 
     sources = [(m_own, w_own, me)] + [(m_got, w_got, peer) for peer in peers]
     strip = 16
@@ -270,20 +292,26 @@
         result[me, here, :] = numer / denom
         return carry
 
-    lax.fori_loop(0, share // strip, strip_step, 0)
-    for k, peer in enumerate(peers):
-        r_copy(peer, k).start()
+    for h in range(HALVES):
+        for peer in peers:
+            for v in range(visits):
+                got_m(peer, v, h).wait_recv()
+        lax.fori_loop(h * half // strip, (h + 1) * half // strip, strip_step, 0)
+        for k, peer in enumerate(peers):
+            r_copy(peer, k, h).start()
     for peer in peers:
-        got_r(peer).wait_recv()
+        for h in range(HALVES):
+            got_r(peer, h).wait_recv()
     for s in range(owners):
         for j in range(mine_blocks):
             out_ref[:, pl.ds((s * mine_blocks + j) * BLOCK, BLOCK)] = result[s, pl.ds(j * rows, rows), :]
 
     for k, peer in enumerate(peers):
         w_copy(peer, k).wait_send()
-        for v in range(visits):
-            m_copy(peer, k, v).wait_send()
-        r_copy(peer, k).wait_send()
+        for h in range(HALVES):
+            for v in range(visits):
+                m_copy(peer, k, v, h).wait_send()
+            r_copy(peer, k, h).wait_send()
 
     @pl.when(has_down)
     def _():
@@ -300,24 +328,19 @@
     visits, rows, cols = exposure.shape
     tiles, owners = lax.axis_size("tile"), lax.axis_size("visit")
     share = cols // BLOCK // owners * rows
-    narrow = 0.5 / (basis_width * basis_width)
-    offsets = jnp.arange(-KHALF, KHALF + 1).astype(jnp.float32)
-    square = (offsets * offsets)[None, None, :]
-    powers = [jnp.ones_like(square), square, square * square]
-    raw = jnp.exp(-square * narrow[:, :, None]) * jnp.stack(
-        [powers[b][:, 0] * ((2.0 * narrow[:, b]) ** b)[:, None] for b in range(BASES)], axis=1
-    )
-    norm = 1.0 / jnp.sum(raw, axis=2)
-    scalars = jnp.concatenate([narrow[:, :, None], norm[:, :, None], spatial_coef], axis=2)
-    scalars = scalars.reshape(visits, BASES * SCALARS)
     f32, dma = jnp.float32, pltpu.SemaphoreType.DMA
     vmem = pl.BlockSpec(memory_space=pltpu.VMEM)
+    smem = pl.BlockSpec(memory_space=pltpu.SMEM)
+    hbm = pl.BlockSpec(memory_space=pl.ANY)
     return pl.pallas_call(
         functools.partial(kernel, tiles, owners),
         out_shape=jax.ShapeDtypeStruct((rows, cols), f32),
-        in_specs=[pl.BlockSpec(memory_space=pltpu.SMEM), vmem, vmem, vmem],
+        in_specs=[smem, smem, hbm, hbm, hbm],
         out_specs=vmem,
         scratch_shapes=[
+            pltpu.VMEM((visits, rows, cols), f32),
+            pltpu.VMEM((visits, rows, cols), f32),
+            pltpu.VMEM((visits, rows, cols), jnp.int32),
             pltpu.VMEM((2, visits, HALO, cols), f32),
             pltpu.VMEM((owners, visits, share, BLOCK), f32),
             pltpu.VMEM((owners, visits, share, BLOCK), f32),
@@ -327,19 +350,22 @@
             pltpu.VMEM((BASES * rows, cols + 2 * SIDE), jnp.bfloat16),
             pltpu.VMEM((owners * share, BLOCK), f32),
             pltpu.VMEM((owners, share, BLOCK), f32),
+            dma(()),
+            dma(()),
+            dma(()),
             dma((2, visits)),
             dma((2, visits)),
             dma((owners,)),
             dma((owners,)),
-            dma((owners, visits)),
-            dma((owners, visits)),
-            dma((owners,)),
-            dma((owners,)),
+            dma((owners, visits, HALVES)),
+            dma((owners, visits, HALVES)),
+            dma((owners, HALVES)),
+            dma((owners, HALVES)),
         ],
         compiler_params=pltpu.CompilerParams(
-            collective_id=0, has_side_effects=True, vmem_limit_bytes=48 * 1024 * 1024
+            collective_id=0, has_side_effects=True, vmem_limit_bytes=56 * 1024 * 1024
         ),
-    )(scalars, exposure, variance, usable)
+    )(basis_width, spatial_coef, exposure, variance, usable)
 
 
 def solution(mesh):

time: 117 us -> 114 us (0.974)
  other arithmetic: 2.64 us -> 0 us
  local copies, waits for them, and re-layouts: 4.38 us -> 3.16 us
    pallas_call x1, Pallas kernels: 109 us -> 110 us  [per_device(): pl.pallas_call(functools.partial(kernel, tiles, owners), out_shape=jax.Sh...]
    unnamed x5 -> x2, local copies, waits for them, and re-layouts: 3.98 us -> 3.16 us
where the time goes in v2:
time: 114 us; the launch traced here: 113 us
  Pallas kernels  110 us (96%)
  local copies, waits for them, and re-layouts  3.16 us (3%)
    pallas_call x1, Pallas kernels, per_device(): pl.pallas_call(functools.partial(kernel, tiles, owners), out_shape=jax.Sh...  110 us
    unnamed x2, local copies, waits for them, and re-layouts  3.16 us

profile of v2, /device:TPU:0, one launch (start us, length us, event | category | flops | bytes accessed | tf_op | source)
XLA Modules:
  0.0 113.5 jit_solution(6147255954290203656)
XLA Ops:
  0.0 1.3 %copy.6.coef_ref = f32[4,3,6]{2,1,0:T(4,128)} copy(f32[4,3,6]{2,0,1:T(4,128)} %param.9) | data formatting | bytes 576 | tf_op args[4]
  1.3 110.3 %shard_map.55 = f32[32,4096]{1,0:T(8,128)} custom-call(f32[4,3]{1,0:T(4,128)} %width_ref.1, f32[4,3,6]{2,1,0:T(4,128)} %copy.6.coef_ref, f32[4,32,4096]{2,1,0:T(8,128)} %expo_hbm.1, f32[4,32,4096]{2,1,0:T(8,128)} %var_hbm.1, s32[4,32,4096]{2,1,0:T(8,128)} %use_hbm.1), custom_call_target="tpu_custom_call" | custom-call | tf_op jit(solution)/shard_map/pallas_call | solution.py:335
  111.6 1.9 %copy.8 = f32[32,4096]{1,0:T(8,128)} copy(f32[32,4096]{1,0:T(8,128)} %shard_map.55) | data formatting | bytes 1048576

commit v3 on v2

--- a/solution.py
+++ b/solution.py
@@ -13,7 +13,7 @@
 HALO = 16
 BLOCK = 256
 SIDE = 128
-HALVES = 2
+HALVES = 4
 MESH = pl.DeviceIdType.MESH
 
 big_value = 1e30
@@ -53,11 +53,18 @@
     has_down = tile < tiles - 1
     far_first = sorted(range(1, owners), key=lambda d: (abs(2 * d - owners), d))
     peers = [lax.rem(me + d, owners) for d in far_first]
-    load_var = pltpu.make_async_copy(var_hbm, var_ref, var_sem)
-    load_use = pltpu.make_async_copy(use_hbm, use_ref, use_sem)
+    def loads(owner):
+        width = mine_blocks * BLOCK
+        there = pl.ds(pl.multiple_of(owner * width, BLOCK), width)
+        return [
+            pltpu.make_async_copy(hbm.at[:, :, there], ref.at[:, :, there], sem.at[owner])
+            for hbm, ref, sem in ((var_hbm, var_ref, var_sem), (use_hbm, use_ref, use_sem))
+        ]
+
     load_expo = pltpu.make_async_copy(expo_hbm, expo_ref, expo_sem)
-    load_var.start()
-    load_use.start()
+    for owner in peers + [me]:
+        for load in loads(owner):
+            load.start()
     load_expo.start()
 
     barrier = pltpu.get_barrier_semaphore()
@@ -72,62 +79,10 @@
     def _():
         pl.semaphore_signal(barrier, inc=1, device_id={"tile": tile + 1}, device_id_type=MESH)
 
-    beside = has_up.astype(jnp.int32) + has_down.astype(jnp.int32)
-    pl.semaphore_wait(barrier, owners - 1 + beside)
-
-    def halo_copy(side, v):
-        start = rows - HALO if side == 0 else 0
-        return pltpu.make_async_remote_copy(
-            src_ref=expo_hbm.at[v, pl.ds(start, HALO), :],
-            dst_ref=halo.at[side, v],
-            send_sem=halo_send.at[side, v],
-            recv_sem=halo_got.at[side, v],
-            device_id={"tile": tile + 1 if side == 0 else tile - 1},
-            device_id_type=MESH,
-        )
-
-    @pl.when(has_down)
-    def _():
-        for v in range(visits):
-            halo_copy(0, v).start()
-
-    @pl.when(has_up)
-    def _():
-        for v in range(visits):
-            halo_copy(1, v).start()
-
-    @pl.when(jnp.logical_not(has_up))
-    def _():
-        halo[0] = jnp.zeros(halo.shape[1:], jnp.float32)
-
-    @pl.when(jnp.logical_not(has_down))
-    def _():
-        halo[1] = jnp.zeros(halo.shape[1:], jnp.float32)
-
-    def w_copy(peer, k):
-        return pltpu.make_async_remote_copy(
-            src_ref=w_own.at[peer], dst_ref=w_got.at[me],
-            send_sem=w_send.at[k], recv_sem=w_recv.at[me],
-            device_id={"visit": peer}, device_id_type=MESH,
-        )
-
-    half = share // HALVES
-
-    def m_copy(peer, k, v, h):
-        return pltpu.make_async_remote_copy(
-            src_ref=m_own.at[peer, v, pl.ds(h * half, half)], dst_ref=m_got.at[me, v, pl.ds(h * half, half)],
-            send_sem=m_send.at[k, v, h], recv_sem=m_recv.at[me, v, h],
-            device_id={"visit": peer}, device_id_type=MESH,
-        )
-
-    def r_copy(peer, k, h):
-        return pltpu.make_async_remote_copy(
-            src_ref=result.at[me, pl.ds(h * half, half)], dst_ref=result.at[me, pl.ds(h * half, half)],
-            send_sem=r_send.at[k, h], recv_sem=r_recv.at[me, h],
-            device_id={"visit": peer}, device_id_type=MESH,
-        )
-
     def weights_for(owner):
+        for load in loads(owner):
+            load.wait()
+
         def step(v, carry):
             for j in range(mine_blocks):
                 first = pl.multiple_of((owner * mine_blocks + j) * BLOCK, BLOCK)
@@ -139,10 +94,65 @@
 
         lax.fori_loop(0, visits, step, 0)
 
-    load_var.wait()
-    load_use.wait()
+    weights_for(peers[0])
+    beside = has_up.astype(jnp.int32) + has_down.astype(jnp.int32)
+    pl.semaphore_wait(barrier, owners - 1 + beside)
+
+    def halo_copy(side, v):
+        start = rows - HALO if side == 0 else 0
+        return pltpu.make_async_remote_copy(
+            src_ref=expo_hbm.at[v, pl.ds(start, HALO), :],
+            dst_ref=halo.at[side, v],
+            send_sem=halo_send.at[side, v],
+            recv_sem=halo_got.at[side, v],
+            device_id={"tile": tile + 1 if side == 0 else tile - 1},
+            device_id_type=MESH,
+        )
+
+    @pl.when(has_down)
+    def _():
+        for v in range(visits):
+            halo_copy(0, v).start()
+
+    @pl.when(has_up)
+    def _():
+        for v in range(visits):
+            halo_copy(1, v).start()
+
+    @pl.when(jnp.logical_not(has_up))
+    def _():
+        halo[0] = jnp.zeros(halo.shape[1:], jnp.float32)
+
+    @pl.when(jnp.logical_not(has_down))
+    def _():
+        halo[1] = jnp.zeros(halo.shape[1:], jnp.float32)
+
+    def w_copy(peer, k):
+        return pltpu.make_async_remote_copy(
+            src_ref=w_own.at[peer], dst_ref=w_got.at[me],
+            send_sem=w_send.at[k], recv_sem=w_recv.at[me],
+            device_id={"visit": peer}, device_id_type=MESH,
+        )
+
+    half = share // HALVES
+
+    def m_copy(peer, k, v, h):
+        return pltpu.make_async_remote_copy(
+            src_ref=m_own.at[peer, v, pl.ds(h * half, half)], dst_ref=m_got.at[me, v, pl.ds(h * half, half)],
+            send_sem=m_send.at[k, v, h], recv_sem=m_recv.at[me, v, h],
+            device_id={"visit": peer}, device_id_type=MESH,
+        )
+
+    def r_copy(peer, k, h):
+        return pltpu.make_async_remote_copy(
+            src_ref=result.at[me, pl.ds(h * half, half)], dst_ref=result.at[me, pl.ds(h * half, half)],
+            send_sem=r_send.at[k, h], recv_sem=r_recv.at[me, h],
+            device_id={"visit": peer}, device_id_type=MESH,
+        )
+
     for k, peer in enumerate(peers):
-        weights_for(peer)
+        if k > 0:
+            weights_for(peer)
         w_copy(peer, k).start()
     weights_for(me)
     load_expo.wait()
@@ -262,7 +272,7 @@
         got_w(peer).wait_recv()
 
     sources = [(m_own, w_own, me)] + [(m_got, w_got, peer) for peer in peers]
-    strip = 16
+    strip = min(16, half)
 
     def strip_step(i, carry):
         here = pl.ds(pl.multiple_of(i * strip, strip), strip)
@@ -351,8 +361,8 @@
             pltpu.VMEM((owners * share, BLOCK), f32),
             pltpu.VMEM((owners, share, BLOCK), f32),
             dma(()),
-            dma(()),
-            dma(()),
+            dma((owners,)),
+            dma((owners,)),
             dma((2, visits)),
             dma((2, visits)),
             dma((owners,)),

time: 114 us -> 115 us (level)
  no operation moved by 1% of the time
where the time goes in v3:
time: 115 us; the launch traced here: 114 us
  Pallas kernels  111 us (97%)
  local copies, waits for them, and re-layouts  3.16 us (3%)
    pallas_call x1, Pallas kernels, per_device(): pl.pallas_call(functools.partial(kernel, tiles, owners), out_shape=jax.Sh...  111 us
    unnamed x2, local copies, waits for them, and re-layouts  3.16 us

profile of v3, /device:TPU:0, one launch (start us, length us, event | category | flops | bytes accessed | tf_op | source)
XLA Modules:
  0.0 114.2 jit_solution(14768307119730514141)
XLA Ops:
  0.0 1.3 %copy.6.coef_ref = f32[4,3,6]{2,1,0:T(4,128)} copy(f32[4,3,6]{2,0,1:T(4,128)} %param.9) | data formatting | bytes 576 | tf_op args[4]
  1.3 111.1 %shard_map.55 = f32[32,4096]{1,0:T(8,128)} custom-call(f32[4,3]{1,0:T(4,128)} %width_ref.1, f32[4,3,6]{2,1,0:T(4,128)} %copy.6.coef_ref, f32[4,32,4096]{2,1,0:T(8,128)} %expo_hbm.1, f32[4,32,4096]{2,1,0:T(8,128)} %var_hbm.1, s32[4,32,4096]{2,1,0:T(8,128)} %use_hbm.1), custom_call_target="tpu_custom_call" | custom-call | tf_op jit(solution)/shard_map/pallas_call | solution.py:345
  112.4 1.9 %copy.8 = f32[32,4096]{1,0:T(8,128)} copy(f32[32,4096]{1,0:T(8,128)} %shard_map.55) | data formatting | bytes 1048576
